TPU v7x, 32 devices: a whole 2x2x4 slice. The times are simulated.
32 devices in a mesh: groups: 2 (over y), strip: 4 (over z), sub: 2 (over x), rep: 2 (over core).
Axes of the slice: x: 2, y: 2, z: 4, core: 2. Of those that a mesh axis runs over, the one named last changes fastest.
Arguments:
- source: bfloat16 [32, 16, 128, 128], P(('groups', 'strip'), 'sub', 'rep'), parts along dimension 0, may hold values from -6 to 6
- target: bfloat16 [32, 16, 128, 128], P(('groups', 'strip'), 'sub', 'rep'), parts along dimension 0, may hold values from -6 to 6
- target_ids: int32 [32, 16, 25], P(('groups', 'strip'), 'sub'), parts along dimension 0, may hold values from 0 to 255, as said below
- out_grad: bfloat16 [32, 16, 25, 128], P(('groups', 'strip'), 'sub'), parts along dimension 0, may hold values from -6 to 6
- w_in: bfloat16 [128, 256], replicated, may hold values from -0.5 to 0.5
- b_in: float32 [256], replicated, may hold values from -4 to 4
- w_out: bfloat16 [256, 128], replicated, may hold values from -0.375 to 0.375
Outputs:
- source_grad: bfloat16 [32, 16, 128, 128], P(('groups', 'strip'), 'sub', 'rep'), parts along dimension 0
- target_grad: bfloat16 [32, 16, 128, 128], P(('groups', 'strip'), 'sub', 'rep'), parts along dimension 0
There are 2 independent parts, one for each index of `groups`. A program takes and returns all parts, laid end to end along the dimension named above; an argument that names none is the same for every part. Nothing has to cross between parts.
Inputs may be any that keep to these rules, and one draw needn't show every extreme that they name: `target_ids`: the targets of source block (i, j) lie within 3 block rows and 3 block columns of it and inside the section; they come in no particular order and may repeat.
All inputs are finite; a program needn't handle non-finite values.
Results may differ from a plain program's by a relative error of at most 0.007.
Values may be sent and summed in bfloat16 or wider, within the bound.
A program may use at most 64 MiB of HBM per device.

v0:
```python
from functools import partial
import math

import jax
import jax.numpy as jnp
from jax import lax
from jax.sharding import PartitionSpec as P

H = 3


def with_halo(cells, sides, width):
    for axis, dim in sides:
        count = lax.axis_size(axis)
        ends = count - 1
        head = lax.slice_in_dim(cells, 0, width, axis=dim)
        tail = lax.slice_in_dim(cells, cells.shape[dim] - width, cells.shape[dim], axis=dim)
        cells = jnp.concatenate(
            [
                lax.ppermute(tail, axis, [(i, (i + 1) % count) for i in range(ends)]),
                cells,
                lax.ppermute(head, axis, [((i + 1) % count, i) for i in range(ends)]),
            ],
            axis=dim,
        )
    return cells


def shifted(x, axis, by):
    peers = lax.axis_size(axis)
    pairs = [(i, i + by) for i in range(peers) if 0 <= i + by < peers]
    return lax.ppermute(x, axis, pairs)


def decoder_grad(cost_block, grad_block, w_in, b_in, w_out):
    count, picks, pixels = cost_block.shape
    cost_rows = cost_block.reshape(count * picks, pixels)
    hidden_pre = jnp.dot(cost_rows, w_in, preferred_element_type=jnp.float32) + b_in
    grad_hidden = lax.dot_general(
        grad_block.reshape(count * picks, pixels),
        w_out,
        (((1,), (1,)), ((), ())),
        preferred_element_type=jnp.float32,
    )
    _, pullback = jax.vjp(partial(jax.nn.gelu, approximate=True), hidden_pre)
    grad_pre = pullback(grad_hidden)[0].astype(jnp.bfloat16)
    grad_cost = lax.dot_general(
        grad_pre, w_in, (((1,), (1,)), ((), ())), preferred_element_type=jnp.float32
    )
    return grad_cost.astype(jnp.bfloat16).reshape(count, picks, pixels)


def shards(source, target, target_ids, out_grad, w_in, b_in, w_out):
    blk_rows, blk_cols, pix_half, channels = source.shape
    picks = target_ids.shape[2]
    rim_width = H
    num_blocks = blk_rows * blk_cols
    inv_root = 1.0 / math.sqrt(channels)
    strip_at = lax.axis_index("strip")
    sub_at = lax.axis_index("sub")
    total_cols = blk_cols * lax.axis_size("sub")
    ext_rows = blk_rows + 2 * rim_width
    ext_cols = blk_cols + 2 * rim_width
    ext_count = ext_rows * ext_cols
    src_flat = source.reshape(num_blocks, pix_half, channels)
    block_ids = target_ids.reshape(num_blocks, picks)
    local_row = block_ids // total_cols - (strip_at * blk_rows - rim_width)
    local_col = block_ids % total_cols - (sub_at * blk_cols - rim_width)
    ext_index = local_row * ext_cols + local_col
    selector = (
        ext_index[:, :, None] == jnp.arange(ext_count, dtype=jnp.int32)[None, None, :]
    ).astype(jnp.float32)
    padded_target = with_halo(target, (("strip", 0), ("sub", 1)), rim_width)
    target_ext = padded_target.reshape(ext_count, pix_half, channels)
    correlation = jnp.einsum(
        "bpc,epc->bep", src_flat, target_ext, preferred_element_type=jnp.float32
    )
    chosen = jnp.take_along_axis(correlation, ext_index[:, :, None], axis=1)
    costs = (chosen * inv_root).astype(jnp.bfloat16)
    grad_local = out_grad.reshape(num_blocks, picks, out_grad.shape[3])
    cost_whole = lax.all_gather(costs, "rep", axis=2, tiled=True)
    dcost_whole = decoder_grad(cost_whole, grad_local, w_in, b_in, w_out)
    grad_cost = lax.dynamic_slice_in_dim(dcost_whole, lax.axis_index("rep") * pix_half, pix_half, 2)
    pair_weight = jnp.einsum(
        "bke,bkp->bep", selector, grad_cost.astype(jnp.float32), precision=lax.Precision.HIGHEST
    ).astype(jnp.bfloat16)
    source_grad = jnp.einsum(
        "bep,epc->bpc", pair_weight, target_ext, preferred_element_type=jnp.float32
    )
    source_grad = (source_grad * inv_root).astype(jnp.bfloat16).reshape(source.shape)
    partial_sum = jnp.einsum(
        "bep,bpc->epc", pair_weight, src_flat, preferred_element_type=jnp.float32
    )
    partial_sum = partial_sum.reshape(ext_rows, ext_cols, pix_half, channels)
    from_before = shifted(
        partial_sum[:, ext_cols - rim_width :].astype(jnp.bfloat16), "sub", 1
    ).astype(jnp.float32)
    from_after = shifted(partial_sum[:, :rim_width].astype(jnp.bfloat16), "sub", -1).astype(
        jnp.float32
    )
    partial_sum = partial_sum.at[:, rim_width : 2 * rim_width].add(from_before)
    partial_sum = partial_sum.at[:, blk_cols : blk_cols + rim_width].add(from_after)
    middle = partial_sum[:, rim_width : rim_width + blk_cols]
    above = shifted(middle[ext_rows - rim_width :].astype(jnp.bfloat16), "strip", 1).astype(
        jnp.float32
    )
    below = shifted(middle[:rim_width].astype(jnp.bfloat16), "strip", -1).astype(jnp.float32)
    middle = middle.at[rim_width : 2 * rim_width].add(above)
    middle = middle.at[blk_rows : blk_rows + rim_width].add(below)
    owned = middle[rim_width : rim_width + blk_rows]
    target_grad = (owned * inv_root).astype(jnp.bfloat16)
    return (source_grad, target_grad)


def solution(mesh):
    placed = (
        P(("groups", "strip"), "sub", "rep", None),
        P(("groups", "strip"), "sub", "rep", None),
        P(("groups", "strip"), "sub", None),
        P(("groups", "strip"), "sub", None, None),
        P(),
        P(),
        P(),
    )
    return jax.shard_map(
        shards,
        mesh=mesh,
        in_specs=placed,
        out_specs=(
            P(("groups", "strip"), "sub", "rep", None),
            P(("groups", "strip"), "sub", "rep", None),
        ),
        check_vma=False,
    )
```

profile of v0, /device:TPU:0, one launch (start us, length us, event | category | flops | bytes accessed | tf_op | source)
XLA Modules:
  0.0 101.5 jit_solution(12239588834286984082)
XLA Ops:
  0.7 1.3 %fusion.76 = (bf16[3,8,64,128]{3,2,1,0:T(8,128)(2,1)S(1)}, bf16[3,8,64,128]{3,2,1,0:T(8,128)(2,1)S(1)}) fusion(bf16[4,8,64,128]{3,2,1,0:T(8,128)(2,1)} %param.16), kind=kLoop, calls=%fused_computation.100 | loop fusion | bytes 1572864 | tf_op jit(solution)/shard_map/slice | solution.py:16
  1.9 5.0 %collective-permute-start = (bf16[3,8,64,128]{3,2,1,0:T(8,128)(2,1)S(1)}, bf16[3,8,64,128]{3,2,1,0:T(8,128)(2,1)S(1)}, u32[]{:S(2)}, u32[]{:S(2)}) collective-permute-start(bf16[3,8,64,128]{3,2,1,0:T(8,128)(2,1)S(1)} %get-tuple-element.67), channel_id=1, source_target_pairs={{0,4},{4,8},{8,12},{1,5},{5,9},{9,13},{2,6},{6,10},{10,14},{3,7},{... | collective-permute-start | bytes 1179656 | tf_op jit(solution)/shard_map/ppermute | solution.py:20
  6.9 1.4 %collective-permute-start.1 = (bf16[3,8,64,128]{3,2,1,0:T(8,128)(2,1)S(1)}, bf16[3,8,64,128]{3,2,1,0:T(8,128)(2,1)S(1)}, u32[]{:S(2)}, u32[]{:S(2)}) collective-permute-start(bf16[3,8,64,128]{3,2,1,0:T(8,128)(2,1)S(1)} %get-tuple-element.66), channel_id=1, source_target_pairs={{4,0},{8,4},{12,8},{5,1},{9,5},{13,9},{6,2},{10,6},{14,10},{7,3},{... | collective-permute-start | bytes 1179656 | tf_op jit(solution)/shard_map/ppermute | solution.py:22
  8.4 6.9 %collective-permute-done = bf16[3,8,64,128]{3,2,1,0:T(8,128)(2,1)S(1)} collective-permute-done((bf16[3,8,64,128]{3,2,1,0:T(8,128)(2,1)S(1)}, bf16[3,8,64,128]{3,2,1,0:T(8,128)(2,1)S(1)}, u32[]{:S(2)}, u32[]{:S(2)}) %collective-permute-start) | collective-permute-done | bytes 393248 | tf_op jit(solution)/shard_map/ppermute | solution.py:20
  15.3 4.2 %collective-permute-done.1 = bf16[3,8,64,128]{3,2,1,0:T(8,128)(2,1)S(1)} collective-permute-done((bf16[3,8,64,128]{3,2,1,0:T(8,128)(2,1)S(1)}, bf16[3,8,64,128]{3,2,1,0:T(8,128)(2,1)S(1)}, u32[]{:S(2)}, u32[]{:S(2)}) %collective-permute-start.1) | collective-permute-done | bytes 393248 | tf_op jit(solution)/shard_map/ppermute | solution.py:22
  19.6 1.0 %fusion.75 = (bf16[10,3,64,128]{3,2,1,0:T(8,128)(2,1)}, bf16[10,3,64,128]{3,2,1,0:T(8,128)(2,1)}) fusion(bf16[10,8,64,128]{3,2,1,0:T(8,128)(2,1)S(1)} %constant_dynamic-update-slice_fusion), kind=kLoop, calls=%fused_computation.99 | loop fusion | bytes 1966080 | tf_op jit(solution)/shard_map/slice | solution.py:17
  20.6 3.4 %collective-permute-start.2 = (bf16[10,3,64,128]{3,2,1,0:T(8,128)(2,1)}, bf16[10,3,64,128]{3,2,1,0:T(8,128)(2,1)S(1)}, u32[]{:S(2)}, u32[]{:S(2)}) collective-permute-start(bf16[10,3,64,128]{3,2,1,0:T(8,128)(2,1)} %get-tuple-element.64), channel_id=1, source_target_pairs={{0,2},{1,3},{4,6},{5,7},{8,10},{9,11},{12,14},{13,15},{16,18},{17,... | collective-permute-start | bytes 1474568 | tf_op jit(solution)/shard_map/ppermute | solution.py:20
  24.0 1.3 %collective-permute-start.3 = (bf16[10,3,64,128]{3,2,1,0:T(8,128)(2,1)}, bf16[10,3,64,128]{3,2,1,0:T(8,128)(2,1)S(1)}, u32[]{:S(2)}, u32[]{:S(2)}) collective-permute-start(bf16[10,3,64,128]{3,2,1,0:T(8,128)(2,1)} %get-tuple-element.65), channel_id=1, source_target_pairs={{2,0},{3,1},{6,4},{7,5},{10,8},{11,9},{14,12},{15,13},{18,16},{19,... | collective-permute-start | bytes 1474568 | tf_op jit(solution)/shard_map/ppermute | solution.py:22
  25.3 0.1 copy.41
  25.5 0.1 reshape.311
  25.6 0.1 copy.45
  25.7 0.1 reshape_reshape.3
  25.8 7.7 %collective-permute-done.2 = bf16[10,3,64,128]{3,2,1,0:T(8,128)(2,1)S(1)} collective-permute-done((bf16[10,3,64,128]{3,2,1,0:T(8,128)(2,1)}, bf16[10,3,64,128]{3,2,1,0:T(8,128)(2,1)S(1)}, u32[]{:S(2)}, u32[]{:S(2)}) %collective-permute-start.2) | collective-permute-done | bytes 491552 | tf_op jit(solution)/shard_map/ppermute | solution.py:20
  33.6 4.0 %collective-permute-done.3 = bf16[10,3,64,128]{3,2,1,0:T(8,128)(2,1)S(1)} collective-permute-done((bf16[10,3,64,128]{3,2,1,0:T(8,128)(2,1)}, bf16[10,3,64,128]{3,2,1,0:T(8,128)(2,1)S(1)}, u32[]{:S(2)}, u32[]{:S(2)}) %collective-permute-start.3) | collective-permute-done | bytes 491552 | tf_op jit(solution)/shard_map/ppermute | solution.py:22
  37.6 0.3 pad_maximum_fusion
  37.9 1.4 %copy-done.1 = bf16[10,14,64,128]{3,2,1,0:T(8,128)(2,1)} copy-done((bf16[10,14,64,128]{3,2,1,0:T(8,128)(2,1)}, bf16[10,14,64,128]{3,2,1,0:T(8,128)(2,1)S(1)}, u32[]{:S(2)}) %copy-start.1) | copy-done | bytes 2293784
  39.3 3.7 %fusion.4 = f32[32,140,64]{1,0,2:T(8,128)} fusion(bf16[140,64,128]{2,1,0:T(8,128)(2,1)S(1)} %bitcast.45, bf16[32,64,128]{2,1,0:T(8,128)(2,1)S(1)} %bitcast.41), kind=kOutput, calls=%fused_computation.7 | convolution fusion | flops 73400320 | bytes 3964928 | tf_op jit(solution)/shard_map/bpc,epc->bep/dot_general | solution.py:75
  43.0 3.3 %copy.49 = f32[32,140,64]{2,0,1:T(8,128)S(1)} copy(f32[32,140,64]{1,0,2:T(8,128)} %fusion.4) | data formatting | bytes 2293760 | tf_op jit(solution)/shard_map/bpc,epc->bep/transpose | solution.py:75
  46.4 9.8 %gather_fusion = f32[800,64]{1,0:T(8,128)S(1)} fusion(f32[32,140,64]{2,0,1:T(8,128)S(1)} %copy.49, s32[800]{0:T(1024)S(1)} %reshape.311), kind=kCustom, calls=%fused_computation | custom fusion | bytes 416000 | tf_op jit(solution)/shard_map/jit(take_along_axis)/gather | solution.py:78
  56.2 0.3 fusion.37
  56.5 0.9 copy.51
  57.5 2.7 %all_gather.3 = bf16[32,25,128]{1,0,2:T(8,128)(2,1)S(1)} all-gather(bf16[32,25,64]{1,0,2:T(8,128)(2,1)S(1)} %copy.51), channel_id=1, replica_groups=mesh['groups'=2,'strip'=4,'sub'=2,'rep'=2] {'rep'}, dimensions={2}, use_global_device_ids=true | all-gather | bytes 307200 | tf_op jit(solution)/shard_map/all_gather | solution.py:81
  60.2 1.9 %reshape.317 = bf16[800,128]{0,1:T(8,128)(2,1)S(1)} reshape(bf16[32,25,128]{1,0,2:T(8,128)(2,1)S(1)} %all_gather.3) | data formatting | bytes 409600 | tf_op jit(solution)/shard_map/reshape | solution.py:37
  62.1 0.3 convolution_add_fusion
  62.4 0.7 convolution_convert_fusion.1
  63.2 0.1 reshape.308
  63.3 0.8 convolution_convert_fusion
  64.0 1.5 %convolution_bitcast_fusion = f32[140,64,128]{2,0,1:T(8,128)S(1)} fusion(bf16[32,140,64]{1,2,0:T(8,128)(2,1)S(1)} %convolution_convert_fusion, bf16[32,64,128]{2,1,0:T(8,128)(2,1)S(1)} %bitcast.42), kind=kOutput, calls=%fused_computation.2 | convolution fusion | flops 73400320 | bytes 5685248 | tf_op jit(solution)/shard_map/bep,bpc->epc/dot_general | solution.py:91
  65.5 1.5 %copy.57 = f32[140,64,128]{2,1,0:T(8,128)S(1)} copy(f32[140,64,128]{2,0,1:T(8,128)S(1)} %convolution_bitcast_fusion) | data formatting | bytes 9175040 | tf_op jit(solution)/shard_map/bep,bpc->epc/transpose | solution.py:91
  67.0 0.6 convert.8
  67.7 1.6 %collective-permute-start.4 = (bf16[10,3,64,128]{3,2,1,0:T(8,128)(2,1)S(1)}, bf16[10,3,64,128]{3,2,1,0:T(8,128)(2,1)S(1)}, u32[]{:S(2)}, u32[]{:S(2)}) collective-permute-start(bf16[10,3,64,128]{3,2,1,0:T(8,128)(2,1)S(1)} %get-tuple-element.63), channel_id=1, source_target_pairs={{0,2},{1,3},{4,6},{5,7},{8,10},{9,11},{12,14},{13,15},{16,18},{17,... | collective-permute-start | bytes 1474568 | tf_op jit(solution)/shard_map/ppermute | solution.py:32
  69.3 1.3 %collective-permute-start.5 = (bf16[10,3,64,128]{3,2,1,0:T(8,128)(2,1)S(1)}, bf16[10,3,64,128]{3,2,1,0:T(8,128)(2,1)S(1)}, u32[]{:S(2)}, u32[]{:S(2)}) collective-permute-start(bf16[10,3,64,128]{3,2,1,0:T(8,128)(2,1)S(1)} %get-tuple-element.62), channel_id=1, source_target_pairs={{2,0},{3,1},{6,4},{7,5},{10,8},{11,9},{14,12},{15,13},{18,16},{19,... | collective-permute-start | bytes 1474568 | tf_op jit(solution)/shard_map/ppermute | solution.py:32
  70.6 9.4 %collective-permute-done.4 = bf16[10,3,64,128]{3,2,1,0:T(8,128)(2,1)S(1)} collective-permute-done((bf16[10,3,64,128]{3,2,1,0:T(8,128)(2,1)S(1)}, bf16[10,3,64,128]{3,2,1,0:T(8,128)(2,1)S(1)}, u32[]{:S(2)}, u32[]{:S(2)}) %collective-permute-start.4) | collective-permute-done | bytes 491552 | tf_op jit(solution)/shard_map/ppermute | solution.py:32
  80.0 0.2 fusion.18
  80.3 3.9 %collective-permute-done.5 = bf16[10,3,64,128]{3,2,1,0:T(8,128)(2,1)S(1)} collective-permute-done((bf16[10,3,64,128]{3,2,1,0:T(8,128)(2,1)S(1)}, bf16[10,3,64,128]{3,2,1,0:T(8,128)(2,1)S(1)}, u32[]{:S(2)}, u32[]{:S(2)}) %collective-permute-start.5) | collective-permute-done | bytes 491552 | tf_op jit(solution)/shard_map/ppermute | solution.py:32
  84.1 0.2 fusion.17
  84.4 0.6 convert.9
  85.0 0.1 fusion.73
  85.1 3.6 %collective-permute-start.6 = (bf16[3,8,64,128]{3,2,1,0:T(8,128)(2,1)S(1)}, bf16[3,8,64,128]{3,2,1,0:T(8,128)(2,1)S(1)}, u32[]{:S(2)}, u32[]{:S(2)}) collective-permute-start(bf16[3,8,64,128]{3,2,1,0:T(8,128)(2,1)S(1)} %get-tuple-element.61), channel_id=1, source_target_pairs={{0,4},{4,8},{8,12},{1,5},{5,9},{9,13},{2,6},{6,10},{10,14},{3,7},{... | collective-permute-start | bytes 1179656 | tf_op jit(solution)/shard_map/ppermute | solution.py:32
  88.7 1.3 %collective-permute-start.7 = (bf16[3,8,64,128]{3,2,1,0:T(8,128)(2,1)S(1)}, bf16[3,8,64,128]{3,2,1,0:T(8,128)(2,1)S(1)}, u32[]{:S(2)}, u32[]{:S(2)}) collective-permute-start(bf16[3,8,64,128]{3,2,1,0:T(8,128)(2,1)S(1)} %get-tuple-element.60), channel_id=1, source_target_pairs={{4,0},{8,4},{12,8},{5,1},{9,5},{13,9},{6,2},{10,6},{14,10},{7,3},{... | collective-permute-start | bytes 1179656 | tf_op jit(solution)/shard_map/ppermute | solution.py:32
  90.0 2.5 %fusion.13 = bf16[4,8,64,128]{3,1,0,2:T(8,128)(2,1)S(1)} fusion(bf16[140,64,128]{2,1,0:T(8,128)(2,1)S(1)} %bitcast.46, bf16[32,140,64]{1,2,0:T(8,128)(2,1)S(1)} %convolution_convert_fusion), kind=kOutput, calls=%fused_computation.12 | convolution fusion | flops 73924608 | bytes 3391488 | tf_op jit(solution)/shard_map/bep,epc->bpc/dot_general | solution.py:87
  92.5 1.0 copy.58
  93.5 0.2 slice.175
  93.7 2.5 %collective-permute-done.6 = bf16[3,8,64,128]{3,2,1,0:T(8,128)(2,1)S(1)} collective-permute-done((bf16[3,8,64,128]{3,2,1,0:T(8,128)(2,1)S(1)}, bf16[3,8,64,128]{3,2,1,0:T(8,128)(2,1)S(1)}, u32[]{:S(2)}, u32[]{:S(2)}) %collective-permute-start.6) | collective-permute-done | bytes 393248 | tf_op jit(solution)/shard_map/ppermute | solution.py:32
  96.2 0.1 fusion.32
  96.3 4.0 %collective-permute-done.7 = bf16[3,8,64,128]{3,2,1,0:T(8,128)(2,1)S(1)} collective-permute-done((bf16[3,8,64,128]{3,2,1,0:T(8,128)(2,1)S(1)}, bf16[3,8,64,128]{3,2,1,0:T(8,128)(2,1)S(1)}, u32[]{:S(2)}, u32[]{:S(2)}) %collective-permute-start.7) | collective-permute-done | bytes 393248 | tf_op jit(solution)/shard_map/ppermute | solution.py:32
  100.3 0.2 fusion.31
  100.5 0.9 fusion.16
  (25 shorter events, 0.4 us)
Async XLA Ops:
  0.6 37.2 %copy-start = (bf16[4,8,64,128]{3,2,1,0:T(8,128)(2,1)S(1)}, bf16[4,8,64,128]{3,2,1,0:T(8,128)(2,1)}, u32[]{:S(2)}) copy-start(bf16[4,8,64,128]{3,2,1,0:T(8,128)(2,1)} %param.15) | copy-start | bytes 1572868
  0.6 14.6 %copy-start.3 = (bf16[4,8,64,128]{3,2,1,0:T(8,128)(2,1)S(1)}, bf16[4,8,64,128]{3,2,1,0:T(8,128)(2,1)}, u32[]{:S(2)}) copy-start(bf16[4,8,64,128]{3,2,1,0:T(8,128)(2,1)} %param.16) | copy-start | bytes 1572868
  1.9 13.3 %collective-permute-start = (bf16[3,8,64,128]{3,2,1,0:T(8,128)(2,1)S(1)}, bf16[3,8,64,128]{3,2,1,0:T(8,128)(2,1)S(1)}, u32[]{:S(2)}, u32[]{:S(2)}) collective-permute-start(bf16[3,8,64,128]{3,2,1,0:T(8,128)(2,1)S(1)} %get-tuple-element.67), channel_id=1, source_target_pairs={{0,4},{4,8},{8,12},{1,5},{5,9},{9,13},{2,6},{6,10},{10,14},{3,7},{... | collective-permute-start | bytes 1179656 | tf_op jit(solution)/shard_map/ppermute | solution.py:20
  6.9 18.4 %copy-start.6 = (s32[4,8,25]{2,1,0:T(8,128)S(1)}, s32[4,8,25]{2,1,0:T(8,128)}, u32[]{:S(2)}) copy-start(s32[4,8,25]{2,1,0:T(8,128)} %param.17) | copy-start | bytes 9604
  6.9 18.8 %copy-start.4 = (bf16[4,8,25,128]{3,1,2,0:T(8,128)(2,1)S(1)}, bf16[4,8,25,128]{3,1,2,0:T(8,128)(2,1)}, u32[]{:S(2)}) copy-start(bf16[4,8,25,128]{3,1,2,0:T(8,128)(2,1)} %param.18) | copy-start | bytes 614404
  6.9 12.6 %collective-permute-start.1 = (bf16[3,8,64,128]{3,2,1,0:T(8,128)(2,1)S(1)}, bf16[3,8,64,128]{3,2,1,0:T(8,128)(2,1)S(1)}, u32[]{:S(2)}, u32[]{:S(2)}) collective-permute-start(bf16[3,8,64,128]{3,2,1,0:T(8,128)(2,1)S(1)} %get-tuple-element.66), channel_id=1, source_target_pairs={{4,0},{8,4},{12,8},{5,1},{9,5},{13,9},{6,2},{10,6},{14,10},{7,3},{... | collective-permute-start | bytes 1179656 | tf_op jit(solution)/shard_map/ppermute | solution.py:22
  20.6 13.0 %collective-permute-start.2 = (bf16[10,3,64,128]{3,2,1,0:T(8,128)(2,1)}, bf16[10,3,64,128]{3,2,1,0:T(8,128)(2,1)S(1)}, u32[]{:S(2)}, u32[]{:S(2)}) collective-permute-start(bf16[10,3,64,128]{3,2,1,0:T(8,128)(2,1)} %get-tuple-element.64), channel_id=1, source_target_pairs={{0,2},{1,3},{4,6},{5,7},{8,10},{9,11},{12,14},{13,15},{16,18},{17,... | collective-permute-start | bytes 1474568 | tf_op jit(solution)/shard_map/ppermute | solution.py:20
  24.0 13.6 %collective-permute-start.3 = (bf16[10,3,64,128]{3,2,1,0:T(8,128)(2,1)}, bf16[10,3,64,128]{3,2,1,0:T(8,128)(2,1)S(1)}, u32[]{:S(2)}, u32[]{:S(2)}) collective-permute-start(bf16[10,3,64,128]{3,2,1,0:T(8,128)(2,1)} %get-tuple-element.65), channel_id=1, source_target_pairs={{2,0},{3,1},{6,4},{7,5},{10,8},{11,9},{14,12},{15,13},{18,16},{19,... | collective-permute-start | bytes 1474568 | tf_op jit(solution)/shard_map/ppermute | solution.py:22
  37.9 1.4 %copy-start.1 = (bf16[10,14,64,128]{3,2,1,0:T(8,128)(2,1)}, bf16[10,14,64,128]{3,2,1,0:T(8,128)(2,1)S(1)}, u32[]{:S(2)}) copy-start(bf16[10,14,64,128]{3,2,1,0:T(8,128)(2,1)S(1)} %pad_maximum_fusion) | copy-start | bytes 6881284
  56.2 5.9 %copy-start.5 = (bf16[128,256]{1,0:T(8,128)(2,1)S(1)}, bf16[128,256]{1,0:T(8,128)(2,1)}, u32[]{:S(2)}) copy-start(bf16[128,256]{1,0:T(8,128)(2,1)} %param.19) | copy-start | bytes 196612
  56.2 5.9 %copy-start.7 = (f32[256]{0:T(256)S(1)}, f32[256]{0:T(256)}, u32[]{:S(2)}) copy-start(f32[256]{0:T(256)} %param.20) | copy-start | bytes 3076
  56.5 5.9 %copy-start.8 = (bf16[256,128]{1,0:T(8,128)(2,1)S(1)}, bf16[256,128]{1,0:T(8,128)(2,1)}, u32[]{:S(2)}) copy-start(bf16[256,128]{1,0:T(8,128)(2,1)} %param.21) | copy-start | bytes 196612
  67.7 12.3 %collective-permute-start.4 = (bf16[10,3,64,128]{3,2,1,0:T(8,128)(2,1)S(1)}, bf16[10,3,64,128]{3,2,1,0:T(8,128)(2,1)S(1)}, u32[]{:S(2)}, u32[]{:S(2)}) collective-permute-start(bf16[10,3,64,128]{3,2,1,0:T(8,128)(2,1)S(1)} %get-tuple-element.63), channel_id=1, source_target_pairs={{0,2},{1,3},{4,6},{5,7},{8,10},{9,11},{12,14},{13,15},{16,18},{17,... | collective-permute-start | bytes 1474568 | tf_op jit(solution)/shard_map/ppermute | solution.py:32
  69.3 14.9 %collective-permute-start.5 = (bf16[10,3,64,128]{3,2,1,0:T(8,128)(2,1)S(1)}, bf16[10,3,64,128]{3,2,1,0:T(8,128)(2,1)S(1)}, u32[]{:S(2)}, u32[]{:S(2)}) collective-permute-start(bf16[10,3,64,128]{3,2,1,0:T(8,128)(2,1)S(1)} %get-tuple-element.62), channel_id=1, source_target_pairs={{2,0},{3,1},{6,4},{7,5},{10,8},{11,9},{14,12},{15,13},{18,16},{19,... | collective-permute-start | bytes 1474568 | tf_op jit(solution)/shard_map/ppermute | solution.py:32
  84.4 5.6 %copy-start.2 = (bf16[10,14,64,128]{3,2,1,0:T(8,128)(2,1)S(1)}, bf16[10,14,64,128]{3,2,1,0:T(8,128)(2,1)}, u32[]{:S(2)}) copy-start(bf16[10,14,64,128]{3,2,1,0:T(8,128)(2,1)} %copy-done.1) | copy-start | bytes 6881284
  85.1 11.1 %collective-permute-start.6 = (bf16[3,8,64,128]{3,2,1,0:T(8,128)(2,1)S(1)}, bf16[3,8,64,128]{3,2,1,0:T(8,128)(2,1)S(1)}, u32[]{:S(2)}, u32[]{:S(2)}) collective-permute-start(bf16[3,8,64,128]{3,2,1,0:T(8,128)(2,1)S(1)} %get-tuple-element.61), channel_id=1, source_target_pairs={{0,4},{4,8},{8,12},{1,5},{5,9},{9,13},{2,6},{6,10},{10,14},{3,7},{... | collective-permute-start | bytes 1179656 | tf_op jit(solution)/shard_map/ppermute | solution.py:32
  88.7 11.6 %collective-permute-start.7 = (bf16[3,8,64,128]{3,2,1,0:T(8,128)(2,1)S(1)}, bf16[3,8,64,128]{3,2,1,0:T(8,128)(2,1)S(1)}, u32[]{:S(2)}, u32[]{:S(2)}) collective-permute-start(bf16[3,8,64,128]{3,2,1,0:T(8,128)(2,1)S(1)} %get-tuple-element.60), channel_id=1, source_target_pairs={{4,0},{8,4},{12,8},{5,1},{9,5},{13,9},{6,2},{10,6},{14,10},{7,3},{... | collective-permute-start | bytes 1179656 | tf_op jit(solution)/shard_map/ppermute | solution.py:32
where the time goes:
time: 102 us; the launch traced here: 101 us
  waiting for transfers between devices  42.7 us (42%)
  local copies, waits for them, and re-layouts  23.2 us (23%)
  starting transfers between devices  18.9 us (19%)
  matrix products  9.48 us (9%)
  other arithmetic  3.45 us (3%)
  blocking collectives  2.74 us (3%)
  between operations  1.03 us (1%)
    ppermute x4, waiting for transfers between devices, shifted(): return lax.ppermute(x, axis, pairs)  19.9 us
    ppermute x2, waiting for transfers between devices, with_halo(): lax.ppermute(tail, axis, [(i, (i + 1) % count) for i in range(ends)])  14.6 us
    gather x3, local copies, waits for them, and re-layouts, shards(): chosen = jnp.take_along_axis(correlation, ext_index[:, :, None], axis=1)  9.9 us
    ppermute x2, starting transfers between devices, with_halo(): lax.ppermute(tail, axis, [(i, (i + 1) % count) for i in range(ends)])  8.37 us
    ppermute x2, waiting for transfers between devices, with_halo(): lax.ppermute(head, axis, [((i + 1) % count, i) for i in range(ends)])  8.21 us
    ppermute x4, starting transfers between devices, shifted(): return lax.ppermute(x, axis, pairs)  7.78 us
    dot_general x1, matrix products, shards(): jnp.einsum('bpc,epc->bep', src_flat, target_ext, preferred_element_type=j...  3.7 us
    transpose x1, local copies, waits for them, and re-layouts, shards(): jnp.einsum('bpc,epc->bep', src_flat, target_ext, preferred_element_type=j...  3.35 us
  transfers between devices with their start and end apart: 8, of which 8 were waited for; matrix products, arithmetic and copies ran while one was open for 4% of the time, Pallas kernels for 0%

commit v1 on v0

v1 whole, which is shorter than its diff:
```python
from functools import partial
import math

import jax
import jax.numpy as jnp
from jax import lax
from jax.experimental import pallas as pl
from jax.experimental.pallas import tpu as pltpu
from jax.sharding import PartitionSpec as P

H = 3
MESH = pl.DeviceIdType.MESH
DIRS = ((-1, 0), (1, 0), (0, -1), (0, 1), (-1, -1), (-1, 1), (1, -1), (1, 1))
ROW_STEP = 4096
F32 = jnp.float32
BF16 = jnp.bfloat16
NT = (((1,), (1,)), ((), ()))


def gelu_slope(x):
    a = math.sqrt(2.0 / math.pi)
    x2 = x * x
    t = jnp.tanh(a * x * (1.0 + 0.044715 * x2))
    return 0.5 * (1.0 + t) + (0.5 * a) * x * (1.0 - t * t) * (1.0 + (3 * 0.044715) * x2)


def cut(step, count, width, lead):
    if step < 0:
        return 0, width, lead + count
    if step > 0:
        return count - width, width, lead - width
    return 0, count, lead


def kernel(cfg, src_ref, tgt_ref, code_ref, og_ref, win_ref, bin_ref, wout_ref,
           sg_ref, tg_ref,
           t_ext, s_ext, t32, s32, corr32, pw32, pwx32, oh_e, oh_m, gh, cst, gc, gext,
           cx, out32, send_sem, recv_sem, local_sem, rep_sem):
    R, CB, PH, C, K, KP, ns, nc = cfg
    J = 128 // KP
    NG = CB // J
    NB = R * CB
    ER, EC = R + 2 * H, CB + 2 * H
    E = ER * EC
    EP = t32.shape[0] // PH
    GC = NG + 2
    SC = GC * J
    G = ER * GC
    HID = win_ref.shape[1]
    inv_root = 1.0 / math.sqrt(C)

    z = lax.axis_index("strip")
    x = lax.axis_index("sub")
    rep = lax.axis_index("rep")
    other = 1 - rep

    def exists(dr, dc):
        ok = jnp.bool_(True)
        if dr < 0:
            ok = jnp.logical_and(ok, z > 0)
        if dr > 0:
            ok = jnp.logical_and(ok, z < ns - 1)
        if dc < 0:
            ok = jnp.logical_and(ok, x > 0)
        if dc > 0:
            ok = jnp.logical_and(ok, x < nc - 1)
        return ok

    def device(dr, dc):
        return {"strip": z + dr, "sub": x + dc}

    barrier = pltpu.get_barrier_semaphore()
    for dr, dc in DIRS:
        @pl.when(exists(dr, dc))
        def _():
            pl.semaphore_signal(barrier, inc=1, device_id=device(dr, dc), device_id_type=MESH)
    pl.semaphore_signal(barrier, inc=1, device_id={"rep": other}, device_id_type=MESH)
    own_t = pltpu.make_async_copy(tgt_ref, t_ext.at[pl.ds(H, R), pl.ds(H, CB)], local_sem.at[0])
    own_t.start()
    own_s = pltpu.make_async_copy(src_ref, s_ext.at[pl.ds(H, R), pl.ds(J, CB)], local_sem.at[1])
    own_s.start()
    rows_n = 1 + (z > 0).astype(jnp.int32) + (z < ns - 1).astype(jnp.int32)
    cols_n = 1 + (x > 0).astype(jnp.int32) + (x < nc - 1).astype(jnp.int32)
    pl.semaphore_wait(barrier, rows_n * cols_n)

    def copy_of(what, d):
        dr, dc = DIRS[d]
        r0, rn, rd = cut(dr, R, H, H)
        if what == 0:
            c0, cn, cd = cut(dc, CB, H, H)
            a, b = tgt_ref.at[pl.ds(r0, rn), pl.ds(c0, cn)], t_ext.at[pl.ds(rd, rn), pl.ds(cd, cn)]
        elif what == 1:
            c0, cn, cd = cut(dc, CB, H, J)
            a, b = src_ref.at[pl.ds(r0, rn), pl.ds(c0, cn)], s_ext.at[pl.ds(rd, rn), pl.ds(cd, cn)]
        elif what == 2:
            a, b = code_ref, cx.at[d]
        else:
            c0, cn, cd = cut(dc, NG, 1, 1)
            a, b = gc.at[pl.ds(r0, rn), pl.ds(c0, cn)], gext.at[pl.ds(rd, rn), pl.ds(cd, cn)]
        return pltpu.make_async_remote_copy(
            src_ref=a, dst_ref=b, send_sem=send_sem.at[what, d], recv_sem=recv_sem.at[what, d],
            device_id=device(dr, dc), device_id_type=MESH)

    def start(what):
        for d, (dr, dc) in enumerate(DIRS):
            @pl.when(exists(dr, dc))
            def _():
                copy_of(what, d).start()

    def wait_send(what):
        for d, (dr, dc) in enumerate(DIRS):
            @pl.when(exists(dr, dc))
            def _():
                copy_of(what, d).wait_send()

    def wait_recv(what):
        for d, (dr, dc) in enumerate(DIRS):
            @pl.when(exists(-dr, -dc))
            def _():
                copy_of(what, d).wait_recv()

    start(2)
    start(0)

    for d, (dr, dc) in enumerate(DIRS):
        @pl.when(jnp.logical_not(exists(-dr, -dc)))
        def _():
            _, rn, rd = cut(dr, R, H, H)
            _, cn, cd = cut(dc, CB, H, H)
            t_ext[pl.ds(rd, rn), pl.ds(cd, cn)] = jnp.zeros((rn, cn, PH, C), BF16)
            _, cn, cd = cut(dc, CB, H, J)
            s_ext[pl.ds(rd, rn), pl.ds(cd, cn)] = jnp.zeros((rn, cn, PH, C), BF16)
            _, cn, cd = cut(dc, NG, 1, 1)
            gext[pl.ds(rd, rn), pl.ds(cd, cn)] = jnp.zeros((rn, cn, PH, J * KP), BF16)
            cx[d] = jnp.full((R, 8, J * KP), 1 << 30, jnp.int32)
    for c in tuple(range(J - H)) + tuple(range(J + CB + H, SC)):
        s_ext[:, c] = jnp.zeros((ER, PH, C), BF16)
    if EP > E:
        t32[pl.ds(E * PH, (EP - E) * PH), :] = jnp.zeros(((EP - E) * PH, C), F32)

    gh[...] = jnp.zeros_like(gh)
    for b in range(NB):
        gh[pl.ds(b * KP, K), :] = lax.dot_general(
            og_ref[b], wout_ref[...], NT, preferred_element_type=F32)

    code_own = code_ref[...].reshape(R * 8, J * KP).T
    lane_e = lax.broadcasted_iota(jnp.int32, (J * KP, EP), 1)
    for r in range(R):
        for h in range(NG):
            col = code_own[:, r * 8 + h:r * 8 + h + 1]
            e = ((col >> 12) - z * R + H) * EC + (col & (ROW_STEP - 1)) - x * CB + H
            oh_e[r * NG + h] = jnp.where(lane_e == e, 1.0, 0.0).astype(BF16)

    wait_recv(2)
    lane_m = lax.broadcasted_iota(jnp.int32, (J * KP, J * NB), 1)
    seat = (lax.broadcasted_iota(jnp.int32, (J * KP, 1), 0) // KP) * NB

    def mark(code_t, r, h, g):
        col = code_t[:, r * 8 + h:r * 8 + h + 1]
        row_m = (col >> 12) - z * R
        col_m = (col & (ROW_STEP - 1)) - x * CB
        inside = (row_m >= 0) & (row_m < R) & (col_m >= 0) & (col_m < CB)
        m = jnp.where(inside, row_m * CB + col_m + seat, -1)
        oh_m[g] = jnp.where(lane_m == m, 1.0, 0.0).astype(BF16)

    for r in range(R):
        for h in range(NG):
            mark(code_own, r, h, (H + r) * GC + 1 + h)
    for d, (dr, dc) in enumerate(DIRS):
        code_t = cx[d].reshape(R * 8, J * KP).T
        r0, rn, rd = cut(dr, R, H, H)
        c0, cn, cd = cut(dc, NG, 1, 1)
        for r in range(rn):
            for h in range(cn):
                mark(code_t, r0 + r, c0 + h, (rd + r) * GC + cd + h)

    own_t.wait()
    own_s.wait()
    wait_send(0)
    start(1)
    wait_recv(0)

    def widen_t(r, _):
        at = pl.multiple_of(r * (EC * PH), EC * PH)
        t32[pl.ds(at, EC * PH), :] = t_ext[r].reshape(EC * PH, C).astype(F32)
        return 0

    lax.fori_loop(0, ER, widen_t, 0)

    def widen_own(r, _):
        at = pl.multiple_of(r * (CB * PH), CB * PH)
        out32[pl.ds(at, CB * PH), :] = s_ext[H + r, pl.ds(J, CB)].reshape(CB * PH, C).astype(F32)
        return 0

    lax.fori_loop(0, R, widen_own, 0)

    def corr_step(p, _):
        s = out32[pl.ds(p, NB, stride=PH), :].astype(BF16)
        t = t32[pl.ds(p, EP, stride=PH), :].astype(BF16)
        full = lax.dot_general(s, t, NT, preferred_element_type=F32) * inv_root
        at = pl.ds(pl.multiple_of(p * NB, NB), NB)
        corr32[0, at, :] = full[:, :128]
        corr32[1, at, :EP - 128] = full[:, 128:]
        return 0

    lax.fori_loop(0, PH, corr_step, 0, unroll=4)

    for b in range(NB):
        at = pl.ds(b, PH, stride=NB)
        lo = corr32[0, at, :].astype(BF16)
        hi = corr32[1, at, :][:, :EP - 128].astype(BF16)
        oh = oh_e[b // J, pl.ds((b % J) * KP, KP), :]
        got = lax.dot_general(oh[:, :128], lo, NT, preferred_element_type=F32)
        got = got + lax.dot_general(oh[:, 128:], hi, NT, preferred_element_type=F32)
        cst[0, pl.ds(b * KP, KP), :] = got.astype(BF16)

    swap = pltpu.make_async_remote_copy(
        src_ref=cst.at[0], dst_ref=cst.at[1], send_sem=rep_sem.at[0], recv_sem=rep_sem.at[1],
        device_id={"rep": other}, device_id_type=MESH)
    swap.start()
    w_mine = win_ref[pl.ds(pl.multiple_of(rep * PH, PH), PH), :]
    w_other = win_ref[pl.ds(pl.multiple_of(other * PH, PH), PH), :]
    swap.wait()

    for r in range(R):
        for h in range(NG):
            at = pl.ds((r * NG + h) * J * KP, J * KP)
            pre = jnp.dot(cst[0, at, :], w_mine, preferred_element_type=F32)
            pre = pre + jnp.dot(cst[1, at, :], w_other, preferred_element_type=F32) + bin_ref[...]
            grad_pre = (gh[at, :] * gelu_slope(pre)).astype(BF16)
            gc[r, h] = lax.dot_general(
                w_mine, grad_pre, NT, preferred_element_type=F32).astype(BF16)
    start(3)

    lane_j = lax.broadcasted_iota(jnp.int32, (PH, J * KP), 1) // KP
    for g in range(R * NG):
        part = gc[g // NG, g % NG]
        stacked = jnp.concatenate(
            [jnp.where(lane_j == j, part, jnp.zeros_like(part)) for j in range(J)], axis=0)
        pw = jnp.dot(stacked, oh_e[g], preferred_element_type=F32).astype(BF16).astype(F32)
        for j in range(J):
            rows = pl.ds(g * J + j, PH, stride=NB)
            piece = pw[j * PH:(j + 1) * PH]
            pw32[0, rows, :] = piece[:, :128]
            pw32[1, rows, :] = jnp.concatenate(
                [piece[:, 128:], jnp.zeros((PH, 256 - EP), F32)], axis=1)

    def source_step(p, _):
        at = pl.ds(pl.multiple_of(p * NB, NB), NB)
        lo = pw32[0, at, :].astype(BF16)
        hi = pw32[1, at, :][:, :EP - 128].astype(BF16)
        t = t32[pl.ds(p, EP, stride=PH), :].astype(BF16)
        out = jnp.dot(lo, t[:128], preferred_element_type=F32)
        out = out + jnp.dot(hi, t[128:], preferred_element_type=F32)
        out32[pl.ds(p, NB, stride=PH), :] = out * inv_root
        return 0

    lax.fori_loop(0, PH, source_step, 0, unroll=4)
    sg_ref[...] = out32[...].astype(BF16).reshape(sg_ref.shape)

    wait_recv(1)

    def widen_s(r, _):
        at = pl.multiple_of(r * (SC * PH), SC * PH)
        s32[pl.ds(at, SC * PH), :] = s_ext[r].reshape(SC * PH, C).astype(F32)
        return 0

    lax.fori_loop(0, ER, widen_s, 0)

    gext[pl.ds(H, R), pl.ds(1, NG)] = gc[...]
    wait_recv(3)
    for g in range(G):
        pwx = jnp.dot(gext[g // GC, g % GC], oh_m[g], preferred_element_type=F32)
        pwx32[pl.ds(g, PH, stride=G), :] = pwx.astype(BF16).astype(F32)

    def target_step(p, _):
        w = pwx32[pl.ds(pl.multiple_of(p * G, G), G), :].T.astype(BF16)
        out = jnp.zeros((NB, C), F32)
        for j in range(J):
            s = s32[pl.ds(j * PH + p, G, stride=J * PH), :].astype(BF16)
            out = out + jnp.dot(w[j * NB:(j + 1) * NB], s, preferred_element_type=F32)
        out32[pl.ds(p, NB, stride=PH), :] = out * inv_root
        return 0

    lax.fori_loop(0, PH, target_step, 0, unroll=4)
    tg_ref[...] = out32[...].astype(BF16).reshape(tg_ref.shape)

    wait_send(1)
    wait_send(2)
    wait_send(3)


def shards(ns, nc, source, target, target_ids, out_grad, w_in, b_in, w_out):
    R, CB, PH, C = source.shape
    K = target_ids.shape[2]
    KP = 32
    J = 128 // KP
    NG = CB // J
    NB = R * CB
    HID = w_in.shape[1]
    ER, EC = R + 2 * H, CB + 2 * H
    E = ER * EC
    EP = -(-E // 16) * 16
    GC = NG + 2
    SC = GC * J
    G = ER * GC
    total_cols = CB * nc
    code = (target_ids // total_cols) * ROW_STEP + target_ids % total_cols
    code = jnp.pad(code, ((0, 0), (0, 0), (0, KP - K)), constant_values=1 << 30)
    code = jnp.pad(code.reshape(R, NG, J * KP), ((0, 0), (0, 8 - NG), (0, 0)),
                   constant_values=1 << 30)
    vmem = pl.BlockSpec(memory_space=pltpu.VMEM)
    hbm = pl.BlockSpec(memory_space=pl.ANY)
    cfg = (R, CB, PH, C, K, KP, ns, nc)
    return pl.pallas_call(
        partial(kernel, cfg),
        out_shape=(jax.ShapeDtypeStruct(source.shape, BF16), jax.ShapeDtypeStruct(target.shape, BF16)),
        in_specs=[hbm, hbm, vmem, vmem, vmem, vmem, vmem],
        out_specs=(vmem, vmem),
        scratch_shapes=[
            pltpu.VMEM((ER, EC, PH, C), BF16),
            pltpu.VMEM((ER, SC, PH, C), BF16),
            pltpu.VMEM((EP * PH, C), F32),
            pltpu.VMEM((ER * SC * PH, C), F32),
            pltpu.VMEM((2, PH * NB, 128), F32),
            pltpu.VMEM((2, PH * NB, 128), F32),
            pltpu.VMEM((PH * G, J * NB), F32),
            pltpu.VMEM((R * NG, J * KP, EP), BF16),
            pltpu.VMEM((G, J * KP, J * NB), BF16),
            pltpu.VMEM((NB * KP, HID), F32),
            pltpu.VMEM((2, NB * KP, PH), BF16),
            pltpu.VMEM((R, NG, PH, J * KP), BF16),
            pltpu.VMEM((ER, GC, PH, J * KP), BF16),
            pltpu.VMEM((8, R, 8, J * KP), jnp.int32),
            pltpu.VMEM((NB * PH, C), F32),
            pltpu.SemaphoreType.DMA((4, 8)),
            pltpu.SemaphoreType.DMA((4, 8)),
            pltpu.SemaphoreType.DMA((2,)),
            pltpu.SemaphoreType.DMA((2,)),
        ],
        compiler_params=pltpu.CompilerParams(
            collective_id=0, has_side_effects=True, vmem_limit_bytes=56 * 1024 * 1024),
    )(source, target, code, out_grad.reshape(NB, K, out_grad.shape[3]), w_in, b_in.reshape(1, HID), w_out)


def solution(mesh):
    placed = (
        P(("groups", "strip"), "sub", "rep", None),
        P(("groups", "strip"), "sub", "rep", None),
        P(("groups", "strip"), "sub", None),
        P(("groups", "strip"), "sub", None, None),
        P(),
        P(),
        P(),
    )
    return jax.shard_map(
        partial(shards, mesh.shape["strip"], mesh.shape["sub"]),
        mesh=mesh,
        in_specs=placed,
        out_specs=(
            P(("groups", "strip"), "sub", "rep", None),
            P(("groups", "strip"), "sub", "rep", None),
        ),
        check_vma=False,
    )
```

time: 102 us -> 51.9 us (0.51)
  Pallas kernels: 0 us -> 45.2 us
  waiting for transfers between devices: 42.7 us -> 0 us
  starting transfers between devices: 18.9 us -> 0 us
  local copies, waits for them, and re-layouts: 23.2 us -> 5.1 us
  matrix products: 9.48 us -> 0 us
  blocking collectives: 2.74 us -> 0 us
  other arithmetic: 3.45 us -> 0.74 us
    pallas_call x0 -> x1, Pallas kernels: none -> 45.2 us  [shards(): pl.pallas_call(partial(kernel, cfg), out_shape=(jax.ShapeDtypeStruct(sour...]
    ppermute x8 -> x0, waiting for transfers between devices: 42.7 us -> none  [the longest x4 19.9 us: shifted(): return lax.ppermute(x, axis, pairs)]
    ppermute x8 -> x0, starting transfers between devices: 18.9 us -> none  [the longest x2 8.37 us: with_halo(): lax.ppermute(tail, axis, [(i, (i + 1) % count) for i in range(ends)])]
    gather x3 -> x0, local copies, waits for them, and re-layouts: 9.9 us -> none  [shards(): chosen = jnp.take_along_axis(correlation, ext_index[:, :, None], axis=1)]
    dot_general x6 -> x0, matrix products: 9.48 us -> none  [the longest x1 3.7 us: shards(): jnp.einsum('bpc,epc->bep', src_flat, target_ext, preferred_element_type=j...]
    transpose x2 -> x0, local copies, waits for them, and re-layouts: 4.82 us -> none  [the longest x1 3.35 us: shards(): jnp.einsum('bpc,epc->bep', src_flat, target_ext, preferred_element_type=j...]
    all_gather x1 -> x0, blocking collectives: 2.74 us -> none  [shards(): cost_whole = lax.all_gather(costs, 'rep', axis=2, tiled=True)]
    slice x5 -> x0, local copies, waits for them, and re-layouts: 2.62 us -> none  [the longest x1 1.27 us: with_halo(): head = lax.slice_in_dim(cells, 0, width, axis=dim)]
  transfers between devices with their start and end apart: 8 -> 0, of which waited for: 8 -> 0; matrix products, arithmetic and copies ran while one was open for 4% -> 0% of each run, Pallas kernels for 0% -> 0%
where the time goes in v1:
time: 51.9 us; the launch traced here: 51.7 us
  Pallas kernels  45.2 us (87%)
  local copies, waits for them, and re-layouts  5.1 us (10%)
  other arithmetic  0.74 us (1%)
  between operations  0.66 us (1%)
    pallas_call x1, Pallas kernels, shards(): pl.pallas_call(partial(kernel, cfg), out_shape=(jax.ShapeDtypeStruct(sour...  45.2 us
    unnamed x5, local copies, waits for them, and re-layouts  4.4 us

profile of v1, /device:TPU:0, one launch (start us, length us, event | category | flops | bytes accessed | tf_op | source)
XLA Modules:
  0.0 51.7 jit_solution(3316723583388303099)
XLA Ops:
  0.6 0.7 %fusion.1 = s32[4,8,25]{2,1,0:T(8,128)S(1)} fusion(s32[4,8,25]{2,1,0:T(8,128)} %param.9), kind=kLoop, calls=%fused_computation.6 | loop fusion | flops 16800 | bytes 6400 | tf_op jit(solution)/shard_map/add | solution.py:308
  1.4 0.1 reshape.13
  1.5 0.6 %pad.9.code_ref = s32[4,8,128]{2,1,0:T(8,128)} pad(s32[4,2,128]{2,1,0:T(2,128)S(1)} %reshape.13, s32[]{:T(128)} %constant.31.clone.1), padding=0_0x0_6x0_0 | pad | bytes 20484 | tf_op jit(solution)/shard_map/jit(_pad)/pad | solution.py:310
  2.1 1.7 %copy.9 = bf16[4,8,25,128]{3,2,1,0:T(8,128)(2,1)} copy(bf16[4,8,25,128]{3,1,2,0:T(8,128)(2,1)} %param.10) | data formatting | bytes 409600 | tf_op args[3]
  3.8 45.2 %shard_map.86 = (bf16[4,8,64,128]{3,2,1,0:T(8,128)(2,1)}, bf16[4,8,64,128]{3,2,1,0:T(8,128)(2,1)}) custom-call(bf16[4,8,64,128]{3,2,1,0:T(8,128)(2,1)} %src_ref.1, bf16[4,8,64,128]{3,2,1,0:T(8,128)(2,1)} %tgt_ref.1, s32[4,8,128]{2,1,0:T(8,128)} %pad.9.code_ref, bf16[32,25,128]{2,1,0:T(8,128)(2,1)} %bitcast.2, bf16[128,256]{1,0:T(8,128)(2,1)} %win_ref.1, ...), custom_call_target="tpu_custom_call" | custom-call | tf_op jit(solution)/shard_map/pallas_call | solution.py:315
  48.9 0.0 copy-start
  48.9 1.9 %copy.12 = bf16[4,8,64,128]{3,2,1,0:T(8,128)(2,1)} copy(bf16[4,8,64,128]{3,2,1,0:T(8,128)(2,1)} %get-tuple-element.4) | data formatting | bytes 1048576
  50.9 0.0 copy-done
  50.9 0.8 %copy.13 = bf16[4,8,64,128]{3,2,1,0:T(8,128)(2,1)} copy(bf16[4,8,64,128]{3,2,1,0:T(8,128)(2,1)S(1)} %copy-done) | data formatting | bytes 1048576
  (1 shorter events, 0.0 us)
Async XLA Ops:
  48.9 1.9 %copy-start = (bf16[4,8,64,128]{3,2,1,0:T(8,128)(2,1)S(1)}, bf16[4,8,64,128]{3,2,1,0:T(8,128)(2,1)}, u32[]{:S(2)}) copy-start(bf16[4,8,64,128]{3,2,1,0:T(8,128)(2,1)} %get-tuple-element.5) | copy-start | bytes 1572868

commit v2 on v1

--- a/solution.py
+++ b/solution.py
@@ -11,7 +11,7 @@
 H = 3
 MESH = pl.DeviceIdType.MESH
 DIRS = ((-1, 0), (1, 0), (0, -1), (0, 1), (-1, -1), (-1, 1), (1, -1), (1, 1))
-ROW_STEP = 4096
+NONE = 1 << 30
 F32 = jnp.float32
 BF16 = jnp.bfloat16
 NT = (((1,), (1,)), ((), ()))
@@ -32,10 +32,18 @@
     return 0, count, lead
 
 
-def kernel(cfg, src_ref, tgt_ref, code_ref, og_ref, win_ref, bin_ref, wout_ref,
+def read_ids(pad_ref, ids, total_cols):
+    rows, picks = ids.shape
+    pad_ref[:, :picks] = ids
+    flat = pad_ref[...].T
+    row = ((flat.astype(F32) + 0.5) * (1.0 / total_cols)).astype(jnp.int32)
+    return row, flat - row * total_cols
+
+
+def kernel(cfg, src_ref, tgt_ref, ids_ref, og_ref, win_ref, bin_ref, wout_ref,
            sg_ref, tg_ref,
            t_ext, s_ext, t32, s32, corr32, pw32, pwx32, oh_e, oh_m, gh, cst, gc, gext,
-           cx, out32, send_sem, recv_sem, local_sem, rep_sem):
+           cx, id_pad, out32, send_sem, recv_sem, gc_send, gc_recv, local_sem, rep_sem):
     R, CB, PH, C, K, KP, ns, nc = cfg
     J = 128 // KP
     NG = CB // J
@@ -92,14 +100,24 @@
         elif what == 1:
             c0, cn, cd = cut(dc, CB, H, J)
             a, b = src_ref.at[pl.ds(r0, rn), pl.ds(c0, cn)], s_ext.at[pl.ds(rd, rn), pl.ds(cd, cn)]
-        elif what == 2:
-            a, b = code_ref, cx.at[d]
         else:
-            c0, cn, cd = cut(dc, NG, 1, 1)
-            a, b = gc.at[pl.ds(r0, rn), pl.ds(c0, cn)], gext.at[pl.ds(rd, rn), pl.ds(cd, cn)]
+            a, b = ids_ref, cx.at[d]
         return pltpu.make_async_remote_copy(
             src_ref=a, dst_ref=b, send_sem=send_sem.at[what, d], recv_sem=recv_sem.at[what, d],
             device_id=device(dr, dc), device_id_type=MESH)
+
+    def gc_copy(d, r):
+        dr, dc = DIRS[d]
+        r0, rn, rd = cut(dr, R, H, H)
+        c0, cn, cd = cut(dc, NG, 1, 1)
+        return pltpu.make_async_remote_copy(
+            src_ref=gc.at[r, pl.ds(c0, cn)], dst_ref=gext.at[rd + r - r0, pl.ds(cd, cn)],
+            send_sem=gc_send.at[d, r], recv_sem=gc_recv.at[d, r],
+            device_id=device(dr, dc), device_id_type=MESH)
+
+    def gc_rows(d):
+        r0, rn, _ = cut(DIRS[d][0], R, H, H)
+        return range(r0, r0 + rn)
 
     def start(what):
         for d, (dr, dc) in enumerate(DIRS):
@@ -132,47 +150,49 @@
             s_ext[pl.ds(rd, rn), pl.ds(cd, cn)] = jnp.zeros((rn, cn, PH, C), BF16)
             _, cn, cd = cut(dc, NG, 1, 1)
             gext[pl.ds(rd, rn), pl.ds(cd, cn)] = jnp.zeros((rn, cn, PH, J * KP), BF16)
-            cx[d] = jnp.full((R, 8, J * KP), 1 << 30, jnp.int32)
+            cx[d] = jnp.full((R, CB, K), NONE, jnp.int32)
     for c in tuple(range(J - H)) + tuple(range(J + CB + H, SC)):
         s_ext[:, c] = jnp.zeros((ER, PH, C), BF16)
     if EP > E:
         t32[pl.ds(E * PH, (EP - E) * PH), :] = jnp.zeros(((EP - E) * PH, C), F32)
 
     gh[...] = jnp.zeros_like(gh)
+    for r in range(R):
+        rows = og_ref[r].astype(F32).reshape(K * CB, og_ref.shape[3]).astype(BF16)
+        out = lax.dot_general(rows, wout_ref[...], NT, preferred_element_type=F32)
+        for k in range(K):
+            piece = out[k * CB:(k + 1) * CB]
+            for q in range(HID // 128):
+                gh[q, pl.ds(r * CB * KP + k, CB, stride=KP), :] = piece[:, q * 128:(q + 1) * 128]
+
+    id_pad[...] = jnp.full(id_pad.shape, NONE, jnp.int32)
+    total_cols = CB * nc
+    own_row, own_col = read_ids(id_pad, ids_ref[...].reshape(NB, K), total_cols)
+    lane_e = lax.broadcasted_iota(jnp.int32, (KP, EP), 1)
+    e_at = (own_row[:KP] - z * R + H) * EC + own_col[:KP] - x * CB + H
     for b in range(NB):
-        gh[pl.ds(b * KP, K), :] = lax.dot_general(
-            og_ref[b], wout_ref[...], NT, preferred_element_type=F32)
-
-    code_own = code_ref[...].reshape(R * 8, J * KP).T
-    lane_e = lax.broadcasted_iota(jnp.int32, (J * KP, EP), 1)
-    for r in range(R):
-        for h in range(NG):
-            col = code_own[:, r * 8 + h:r * 8 + h + 1]
-            e = ((col >> 12) - z * R + H) * EC + (col & (ROW_STEP - 1)) - x * CB + H
-            oh_e[r * NG + h] = jnp.where(lane_e == e, 1.0, 0.0).astype(BF16)
+        oh_e[b // J, pl.ds((b % J) * KP, KP), :] = jnp.where(
+            lane_e == e_at[:, b:b + 1], 1.0, 0.0).astype(BF16)
 
     wait_recv(2)
-    lane_m = lax.broadcasted_iota(jnp.int32, (J * KP, J * NB), 1)
-    seat = (lax.broadcasted_iota(jnp.int32, (J * KP, 1), 0) // KP) * NB
-
-    def mark(code_t, r, h, g):
-        col = code_t[:, r * 8 + h:r * 8 + h + 1]
-        row_m = (col >> 12) - z * R
-        col_m = (col & (ROW_STEP - 1)) - x * CB
+    lane_m = lax.broadcasted_iota(jnp.int32, (KP, J * NB), 1)
+
+    def mark(row, col, r0, rn, rd, c0, cn, cd):
+        row_m = row[:KP] - z * R
+        col_m = col[:KP] - x * CB
         inside = (row_m >= 0) & (row_m < R) & (col_m >= 0) & (col_m < CB)
-        m = jnp.where(inside, row_m * CB + col_m + seat, -1)
-        oh_m[g] = jnp.where(lane_m == m, 1.0, 0.0).astype(BF16)
-
-    for r in range(R):
-        for h in range(NG):
-            mark(code_own, r, h, (H + r) * GC + 1 + h)
-    for d, (dr, dc) in enumerate(DIRS):
-        code_t = cx[d].reshape(R * 8, J * KP).T
-        r0, rn, rd = cut(dr, R, H, H)
-        c0, cn, cd = cut(dc, NG, 1, 1)
+        m = jnp.where(inside, row_m * CB + col_m, -J * NB)
         for r in range(rn):
             for h in range(cn):
-                mark(code_t, r0 + r, c0 + h, (rd + r) * GC + cd + h)
+                for j in range(J):
+                    b = (r0 + r) * CB + (c0 + h) * J + j
+                    oh_m[(rd + r) * GC + cd + h, pl.ds(j * KP, KP), :] = jnp.where(
+                        lane_m == m[:, b:b + 1] + j * NB, 1.0, 0.0).astype(BF16)
+
+    mark(own_row, own_col, 0, R, H, 0, NG, 1)
+    for d, (dr, dc) in enumerate(DIRS):
+        row, col = read_ids(id_pad, cx[d].reshape(NB, K), total_cols)
+        mark(row, col, *cut(dr, R, H, H), *cut(dc, NG, 1, 1))
 
     own_t.wait()
     own_s.wait()
@@ -203,7 +223,14 @@
         corr32[1, at, :EP - 128] = full[:, 128:]
         return 0
 
-    lax.fori_loop(0, PH, corr_step, 0, unroll=4)
+    lax.fori_loop(0, PH, corr_step, 0, unroll=16)
+
+    def swap(r):
+        at = pl.ds(r * CB * KP, CB * KP)
+        return pltpu.make_async_remote_copy(
+            src_ref=cst.at[0, at], dst_ref=cst.at[1, at],
+            send_sem=rep_sem.at[0, r], recv_sem=rep_sem.at[1, r],
+            device_id={"rep": other}, device_id_type=MESH)
 
     for b in range(NB):
         at = pl.ds(b, PH, stride=NB)
@@ -213,24 +240,27 @@
         got = lax.dot_general(oh[:, :128], lo, NT, preferred_element_type=F32)
         got = got + lax.dot_general(oh[:, 128:], hi, NT, preferred_element_type=F32)
         cst[0, pl.ds(b * KP, KP), :] = got.astype(BF16)
-
-    swap = pltpu.make_async_remote_copy(
-        src_ref=cst.at[0], dst_ref=cst.at[1], send_sem=rep_sem.at[0], recv_sem=rep_sem.at[1],
-        device_id={"rep": other}, device_id_type=MESH)
-    swap.start()
+        if (b + 1) % CB == 0:
+            swap(b // CB).start()
+
     w_mine = win_ref[pl.ds(pl.multiple_of(rep * PH, PH), PH), :]
     w_other = win_ref[pl.ds(pl.multiple_of(other * PH, PH), PH), :]
-    swap.wait()
 
     for r in range(R):
+        swap(r).wait()
         for h in range(NG):
             at = pl.ds((r * NG + h) * J * KP, J * KP)
             pre = jnp.dot(cst[0, at, :], w_mine, preferred_element_type=F32)
             pre = pre + jnp.dot(cst[1, at, :], w_other, preferred_element_type=F32) + bin_ref[...]
-            grad_pre = (gh[at, :] * gelu_slope(pre)).astype(BF16)
+            up = jnp.concatenate([gh[q, at, :] for q in range(HID // 128)], axis=1)
+            grad_pre = (up * gelu_slope(pre)).astype(BF16)
             gc[r, h] = lax.dot_general(
                 w_mine, grad_pre, NT, preferred_element_type=F32).astype(BF16)
-    start(3)
+        for d in reversed(range(len(DIRS))):
+            if r in gc_rows(d):
+                @pl.when(exists(*DIRS[d]))
+                def _():
+                    gc_copy(d, r).start()
 
     lane_j = lax.broadcasted_iota(jnp.int32, (PH, J * KP), 1) // KP
     for g in range(R * NG):
@@ -255,7 +285,7 @@
         out32[pl.ds(p, NB, stride=PH), :] = out * inv_root
         return 0
 
-    lax.fori_loop(0, PH, source_step, 0, unroll=4)
+    lax.fori_loop(0, PH, source_step, 0, unroll=16)
     sg_ref[...] = out32[...].astype(BF16).reshape(sg_ref.shape)
 
     wait_recv(1)
@@ -268,7 +298,11 @@
     lax.fori_loop(0, ER, widen_s, 0)
 
     gext[pl.ds(H, R), pl.ds(1, NG)] = gc[...]
-    wait_recv(3)
+    for d, (dr, dc) in enumerate(DIRS):
+        @pl.when(exists(-dr, -dc))
+        def _():
+            for r in gc_rows(d):
+                gc_copy(d, r).wait_recv()
     for g in range(G):
         pwx = jnp.dot(gext[g // GC, g % GC], oh_m[g], preferred_element_type=F32)
         pwx32[pl.ds(g, PH, stride=G), :] = pwx.astype(BF16).astype(F32)
@@ -282,12 +316,16 @@
         out32[pl.ds(p, NB, stride=PH), :] = out * inv_root
         return 0
 
-    lax.fori_loop(0, PH, target_step, 0, unroll=4)
+    lax.fori_loop(0, PH, target_step, 0, unroll=16)
     tg_ref[...] = out32[...].astype(BF16).reshape(tg_ref.shape)
 
     wait_send(1)
     wait_send(2)
-    wait_send(3)
+    for d, (dr, dc) in enumerate(DIRS):
+        @pl.when(exists(dr, dc))
+        def _():
+            for r in gc_rows(d):
+                gc_copy(d, r).wait_send()
 
 
 def shards(ns, nc, source, target, target_ids, out_grad, w_in, b_in, w_out):
@@ -304,11 +342,6 @@
     GC = NG + 2
     SC = GC * J
     G = ER * GC
-    total_cols = CB * nc
-    code = (target_ids // total_cols) * ROW_STEP + target_ids % total_cols
-    code = jnp.pad(code, ((0, 0), (0, 0), (0, KP - K)), constant_values=1 << 30)
-    code = jnp.pad(code.reshape(R, NG, J * KP), ((0, 0), (0, 8 - NG), (0, 0)),
-                   constant_values=1 << 30)
     vmem = pl.BlockSpec(memory_space=pltpu.VMEM)
     hbm = pl.BlockSpec(memory_space=pl.ANY)
     cfg = (R, CB, PH, C, K, KP, ns, nc)
@@ -327,20 +360,23 @@
             pltpu.VMEM((PH * G, J * NB), F32),
             pltpu.VMEM((R * NG, J * KP, EP), BF16),
             pltpu.VMEM((G, J * KP, J * NB), BF16),
-            pltpu.VMEM((NB * KP, HID), F32),
+            pltpu.VMEM((HID // 128, NB * KP, 128), F32),
             pltpu.VMEM((2, NB * KP, PH), BF16),
             pltpu.VMEM((R, NG, PH, J * KP), BF16),
             pltpu.VMEM((ER, GC, PH, J * KP), BF16),
-            pltpu.VMEM((8, R, 8, J * KP), jnp.int32),
+            pltpu.VMEM((8, R, CB, K), jnp.int32),
+            pltpu.VMEM((NB, 128), jnp.int32),
             pltpu.VMEM((NB * PH, C), F32),
-            pltpu.SemaphoreType.DMA((4, 8)),
-            pltpu.SemaphoreType.DMA((4, 8)),
+            pltpu.SemaphoreType.DMA((3, 8)),
+            pltpu.SemaphoreType.DMA((3, 8)),
+            pltpu.SemaphoreType.DMA((8, R)),
+            pltpu.SemaphoreType.DMA((8, R)),
             pltpu.SemaphoreType.DMA((2,)),
-            pltpu.SemaphoreType.DMA((2,)),
+            pltpu.SemaphoreType.DMA((2, R)),
         ],
         compiler_params=pltpu.CompilerParams(
             collective_id=0, has_side_effects=True, vmem_limit_bytes=56 * 1024 * 1024),
-    )(source, target, code, out_grad.reshape(NB, K, out_grad.shape[3]), w_in, b_in.reshape(1, HID), w_out)
+    )(source, target, target_ids, out_grad.transpose(0, 2, 1, 3), w_in, b_in.reshape(1, HID), w_out)
 
 
 def solution(mesh):

time: 51.9 us -> 44.8 us (0.86); the launches traced: 51.7 us -> 43.9 us
  Pallas kernels: 45.2 us -> 40.6 us
  local copies, waits for them, and re-layouts: 5.1 us -> 2.72 us
  other arithmetic: 0.74 us -> 0 us
    pallas_call x1, Pallas kernels: 45.2 us -> 40.6 us  [shards(): pl.pallas_call(partial(kernel, cfg), out_shape=(jax.ShapeDtypeStruct(sour...]
    unnamed x5 -> x4, local copies, waits for them, and re-layouts: 4.4 us -> 2.72 us
    add x1 -> x0, other arithmetic: 0.74 us -> none  [shards(): code = target_ids // total_cols * ROW_STEP + target_ids % total_cols]
    pad x2 -> x0, local copies, waits for them, and re-layouts: 0.62 us -> none  [the longest x1 0.61 us: shards(): jnp.pad(code.reshape(R, NG, J * KP), ((0, 0), (0, 8 - NG), (0, 0)), const...]
where the time goes in v2:
time: 44.8 us; the launch traced here: 43.9 us
  Pallas kernels  40.6 us (91%)
  local copies, waits for them, and re-layouts  2.72 us (6%)
  between operations  0.65 us (1%)
    pallas_call x1, Pallas kernels, shards(): pl.pallas_call(partial(kernel, cfg), out_shape=(jax.ShapeDtypeStruct(sour...  40.6 us
    unnamed x4, local copies, waits for them, and re-layouts  2.72 us

profile of v2, /device:TPU:0, one launch (start us, length us, event | category | flops | bytes accessed | tf_op | source)
XLA Modules:
  0.0 43.9 jit_solution(4573220607395758202)
XLA Ops:
  0.6 40.6 %shard_map.86 = (bf16[4,8,64,128]{3,2,1,0:T(8,128)(2,1)}, bf16[4,8,64,128]{3,2,1,0:T(8,128)(2,1)}) custom-call(bf16[4,8,64,128]{3,2,1,0:T(8,128)(2,1)} %src_ref.1, bf16[4,8,64,128]{3,2,1,0:T(8,128)(2,1)} %tgt_ref.1, s32[4,8,25]{2,1,0:T(8,128)} %ids_ref.1, bf16[4,25,8,128]{3,2,1,0:T(8,128)(2,1)} %bitcast.2, bf16[128,256]{1,0:T(8,128)(2,1)} %win_ref.1, ...), custom_call_target="tpu_custom_call" | custom-call | tf_op jit(solution)/shard_map/pallas_call | solution.py:348
  41.2 0.0 copy-start
  41.2 1.9 %copy.11 = bf16[4,8,64,128]{3,2,1,0:T(8,128)(2,1)} copy(bf16[4,8,64,128]{3,2,1,0:T(8,128)(2,1)} %get-tuple-element.4) | data formatting | bytes 1048576
  43.1 0.0 copy-done
  43.1 0.8 %copy.12 = bf16[4,8,64,128]{3,2,1,0:T(8,128)(2,1)} copy(bf16[4,8,64,128]{3,2,1,0:T(8,128)(2,1)S(1)} %copy-done) | data formatting | bytes 1048576
Async XLA Ops:
  41.2 1.9 %copy-start = (bf16[4,8,64,128]{3,2,1,0:T(8,128)(2,1)S(1)}, bf16[4,8,64,128]{3,2,1,0:T(8,128)(2,1)}, u32[]{:S(2)}) copy-start(bf16[4,8,64,128]{3,2,1,0:T(8,128)(2,1)} %get-tuple-element.5) | copy-start | bytes 1572868

commit v3 on v2

--- a/solution.py
+++ b/solution.py
@@ -288,6 +288,14 @@
     lax.fori_loop(0, PH, source_step, 0, unroll=16)
     sg_ref[...] = out32[...].astype(BF16).reshape(sg_ref.shape)
 
+    def pair_weights(g, part):
+        pwx = jnp.dot(part, oh_m[g], preferred_element_type=F32)
+        pwx32[pl.ds(g, PH, stride=G), :] = pwx.astype(BF16).astype(F32)
+
+    own_groups = [(H + r) * GC + 1 + h for r in range(R) for h in range(NG)]
+    for i, g in enumerate(own_groups):
+        pair_weights(g, gc[i // NG, i % NG])
+
     wait_recv(1)
 
     def widen_s(r, _):
@@ -297,15 +305,14 @@
 
     lax.fori_loop(0, ER, widen_s, 0)
 
-    gext[pl.ds(H, R), pl.ds(1, NG)] = gc[...]
     for d, (dr, dc) in enumerate(DIRS):
         @pl.when(exists(-dr, -dc))
         def _():
             for r in gc_rows(d):
                 gc_copy(d, r).wait_recv()
     for g in range(G):
-        pwx = jnp.dot(gext[g // GC, g % GC], oh_m[g], preferred_element_type=F32)
-        pwx32[pl.ds(g, PH, stride=G), :] = pwx.astype(BF16).astype(F32)
+        if g not in own_groups:
+            pair_weights(g, gext[g // GC, g % GC])
 
     def target_step(p, _):
         w = pwx32[pl.ds(pl.multiple_of(p * G, G), G), :].T.astype(BF16)
@@ -316,7 +323,7 @@
         out32[pl.ds(p, NB, stride=PH), :] = out * inv_root
         return 0
 
-    lax.fori_loop(0, PH, target_step, 0, unroll=16)
+    lax.fori_loop(0, PH, target_step, 0, unroll=32)
     tg_ref[...] = out32[...].astype(BF16).reshape(tg_ref.shape)
 
     wait_send(1)

time: 44.8 us -> 44.4 us (level)
  no operation moved by 1% of the time
where the time goes in v3:
time: 44.4 us; the launch traced here: 43.6 us
  Pallas kernels  40.2 us (91%)
  local copies, waits for them, and re-layouts  2.72 us (6%)
  between operations  0.65 us (1%)
    pallas_call x1, Pallas kernels, shards(): pl.pallas_call(partial(kernel, cfg), out_shape=(jax.ShapeDtypeStruct(sour...  40.2 us
    unnamed x4, local copies, waits for them, and re-layouts  2.72 us

profile of v3, /device:TPU:0, one launch (start us, length us, event | category | flops | bytes accessed | tf_op | source)
XLA Modules:
  0.0 43.6 jit_solution(5598479479797729695)
XLA Ops:
  0.6 40.2 %shard_map.86 = (bf16[4,8,64,128]{3,2,1,0:T(8,128)(2,1)}, bf16[4,8,64,128]{3,2,1,0:T(8,128)(2,1)}) custom-call(bf16[4,8,64,128]{3,2,1,0:T(8,128)(2,1)} %src_ref.1, bf16[4,8,64,128]{3,2,1,0:T(8,128)(2,1)} %tgt_ref.1, s32[4,8,25]{2,1,0:T(8,128)} %ids_ref.1, bf16[4,25,8,128]{3,2,1,0:T(8,128)(2,1)} %bitcast.2, bf16[128,256]{1,0:T(8,128)(2,1)} %win_ref.1, ...), custom_call_target="tpu_custom_call" | custom-call | tf_op jit(solution)/shard_map/pallas_call | solution.py:355
  40.9 0.0 copy-start
  40.9 1.9 %copy.11 = bf16[4,8,64,128]{3,2,1,0:T(8,128)(2,1)} copy(bf16[4,8,64,128]{3,2,1,0:T(8,128)(2,1)} %get-tuple-element.4) | data formatting | bytes 1048576
  42.8 0.0 copy-done
  42.8 0.8 %copy.12 = bf16[4,8,64,128]{3,2,1,0:T(8,128)(2,1)} copy(bf16[4,8,64,128]{3,2,1,0:T(8,128)(2,1)S(1)} %copy-done) | data formatting | bytes 1048576
Async XLA Ops:
  40.9 1.9 %copy-start = (bf16[4,8,64,128]{3,2,1,0:T(8,128)(2,1)S(1)}, bf16[4,8,64,128]{3,2,1,0:T(8,128)(2,1)}, u32[]{:S(2)}) copy-start(bf16[4,8,64,128]{3,2,1,0:T(8,128)(2,1)} %get-tuple-element.5) | copy-start | bytes 1572868
